TPU v7x, 256 devices: a whole 4x4x8 slice. The times are simulated.
256 devices in a mesh: pair: 32 (over y, z_lo, core), win: 8 (over x, z_hi).
Axes of the slice: x: 4, y: 4, z: 8 (z_hi: 2, z_lo: 4; z = z_hi * 4 + z_lo), core: 2. Of those that a mesh axis runs over, the one named last changes fastest.
Arguments:
- traces: bfloat16 [4096, 256, 1024], P('pair', 'win'), may hold values from -6 to 6
- taps: float32 [64], replicated, may hold values from -0.5 to 0.5
- alive: int32 [4096], P('pair'), may hold values 0 or 1
Outputs:
- cross: bfloat16 [2, 2, 256, 4096, 128], P(None, None, 'win', 'pair')
All inputs are finite; a program needn't handle non-finite values. No bound on the sum of `alive` on one device may be relied on, other than what follows from the above.
Results may differ from a plain program's by a relative error of at most 0.0071.
Values may be sent and summed in bfloat16 or wider, within the bound.
A program may use at most 128 MiB of HBM per device.

v0:
```python
import math

import jax
import jax.numpy as jnp
from jax import lax
from jax.sharding import PartitionSpec as P

BINS = 256


def passed_along(block, axis, distance):
    devices = range(lax.axis_size(axis))
    route = [(i - distance, i) for i in devices if i - distance in devices]
    return lax.ppermute(block, axis, route)


def shifted(value, axis, steps):
    count = lax.axis_size(axis)
    pairs = [(source, (source + steps) % count) for source in range(count)]
    return lax.ppermute(value, axis, pairs)


def filtered_basis(taps, samples, bins):
    ntaps = taps.shape[0]
    length = samples + ntaps
    sample_index = jnp.arange(samples, dtype=jnp.int32)[:, None]
    bin_index = jnp.arange(bins, dtype=jnp.int32)[None, :]
    phase = (sample_index * bin_index % samples).astype(jnp.float32) * (2.0 * math.pi / samples)
    scale = 1.0 / math.sqrt(samples)
    plain = jnp.concatenate([jnp.cos(phase), -jnp.sin(phase)], axis=1) * scale
    period = 2 * samples + ntaps
    pattern = jnp.concatenate([jnp.zeros((period - ntaps,), jnp.float32), taps])
    tiled = jnp.tile(pattern, length)[: length * (period - 1)]
    filt = tiled.reshape(length, period - 1)[:, :samples]
    total = jnp.dot(
        filt, plain, preferred_element_type=jnp.float32, precision=lax.Precision.HIGHEST
    )
    return total.astype(jnp.bfloat16)


def cross_block(mine, other, norm):
    mine_re = mine[0]
    mine_im = mine[1]
    other_re = other[0]
    other_im = other[1]
    real_part = jnp.einsum("fis,fjs->fij", mine_re, other_re, preferred_element_type=jnp.float32)
    real_part = real_part + jnp.einsum(
        "fis,fjs->fij", mine_im, other_im, preferred_element_type=jnp.float32
    )
    imag_part = jnp.einsum("fis,fjs->fij", mine_im, other_re, preferred_element_type=jnp.float32)
    imag_part = imag_part - jnp.einsum(
        "fis,fjs->fij", mine_re, other_im, preferred_element_type=jnp.float32
    )
    return (jnp.stack([real_part, imag_part], 0) * norm).astype(jnp.bfloat16)


def per_device(traces, taps, alive):
    channels, subs, samples = traces.shape
    ntaps = taps.shape[0]
    length = samples + ntaps
    nwin = lax.axis_size("win")
    npair = lax.axis_size("pair")
    bins = BINS
    share = bins // nwin
    basis = filtered_basis(taps, samples, bins)
    basis = basis.reshape(length, 2, nwin, share).transpose(0, 2, 1, 3).reshape(length, 2 * bins)
    basis_rows = basis.T
    tail = traces[:, subs - 1, samples - ntaps :]
    before = passed_along(tail, "win", 1)
    prior = jnp.concatenate([before[:, None, :], traces[:, :-1, samples - ntaps :]], axis=1)
    extended = jnp.concatenate([prior, traces], axis=2)
    product = jnp.einsum("qt,cst->qcs", basis_rows, extended, preferred_element_type=jnp.float32)
    product = product * alive.astype(jnp.float32)[None, :, None]
    spectra = product.astype(jnp.bfloat16).reshape(nwin, 2, share, channels, subs)
    norm = 1.0 / math.sqrt(subs * nwin)
    offsets = (1, npair // 2)
    results = []
    own = lax.all_to_all(spectra, "win", split_axis=0, concat_axis=4, tiled=True)
    own = own.reshape(2, share, channels, subs * nwin)
    for offset in offsets:
        other = shifted(own, "pair", offset)
        results.append(cross_block(own, other, norm))
    return jnp.stack(results, axis=1)


def solution(mesh):
    placed = (P("pair", "win", None), P(), P("pair"))
    return jax.shard_map(
        per_device,
        mesh=mesh,
        in_specs=placed,
        out_specs=P(None, None, "win", "pair", None),
        check_vma=False,
    )
```

profile of v0, /device:TPU:1, one launch (start us, length us, event | category | flops | bytes accessed | tf_op | source)
XLA Modules:
  0.0 303.8 jit_solution(18325649808654107415)
XLA Ops:
  0.0 12.1 %copy.30 = bf16[128,32,1024]{0,2,1:T(8,128)(2,1)} copy(bf16[128,32,1024]{2,1,0:T(8,128)(2,1)} %param.3) | data formatting | bytes 16777216 | tf_op args[0]
  12.8 9.6 %collective-permute-start = (bf16[128,64]{0,1:T(8,128)(2,1)S(1)}, bf16[128,64]{0,1:T(8,128)(2,1)S(1)}, u32[]{:S(2)}, u32[]{:S(2)}) collective-permute-start(bf16[128,64]{0,1:T(8,128)(2,1)S(1)} %slice_bitcast_fusion.20), channel_id=1, source_target_pairs={{0,1},{1,2},{2,3},{3,4},{4,5},{5,6},{6,7},{8,9},{9,10},{10,11},{11... | collective-permute-start | bytes 49160 | tf_op jit(solution)/shard_map/ppermute | solution.py:14
  22.5 4.1 %sine_negate_fusion = (f32[1024,256]{1,0:T(8,128)S(1)}, f32[1024,256]{1,0:T(8,128)S(1)}) fusion(), kind=kLoop, calls=%fused_computation.41 | loop fusion | flops 3932160 | bytes 2097152 | tf_op jit(solution)/shard_map/neg | solution.py:30
  26.6 4.3 %tile.4 = f32[1088,2112]{1,0:T(8,128)} broadcast(f32[2112]{0:T(1024)S(1)} %concatenate.26), dimensions={1} | broadcast | bytes 9199872 | tf_op jit(solution)/shard_map/tile | solution.py:33
  30.9 11.6 %tile.10 = f32[2297856]{0:T(1024)} reshape(f32[1088,2112]{1,0:T(8,128)} %tile.4) | data formatting | bytes 18382848 | tf_op jit(solution)/shard_map/tile | solution.py:33
  42.5 8.3 %slice.44 = f32[2296768]{0:T(1024)} slice(f32[2297856]{0:T(1024)} %tile.10), slice={[0:2296768]} | slice | bytes 18374144 | tf_op jit(solution)/shard_map/slice | solution.py:33
  50.8 15.5 %reshape.90 = f32[1088,2111]{1,0:T(8,128)} reshape(f32[2296768]{0:T(1024)} %slice.44) | data formatting | bytes 18374144 | tf_op jit(solution)/shard_map/reshape | solution.py:34
  66.3 9.1 %fusion.12 = bf16[1088,512]{1,0:T(8,128)(2,1)S(1)} fusion(f32[1088,2111]{1,0:T(8,128)} %reshape.90, f32[1024,256]{1,0:T(8,128)S(1)} %get-tuple-element.9, f32[1024,256]{1,0:T(8,128)S(1)} %get-tuple-element.10), kind=kOutput, calls=%fused_computation.14 | convolution fusion | flops 6846709760 | bytes 7667712 | tf_op jit(solution)/shard_map/dot_general | solution.py:35
  75.4 1.1 slice.47
  77.3 8.4 %multiply_convert_fusion = bf16[512,128,32]{1,0,2:T(8,128)(2,1)S(1)} fusion(f32[128]{0:T(128)S(1)} %convert_element_type.36, bf16[1088,512,1]{0,1,2:T(8,128)(2,1)S(1)} %bitcast.71, bf16[128,32,1024]{0,2,1:T(8,128)(2,1)} %copy.30, bf16[128,31,64]{0,2,1:T(8,128)(2,1)S(1)} %slice.47, bf16[128,1,64]{0,2,1:T(8,128)(2,1)S(1)} %bitcast.72), kind=kOutput, calls=%fused_computation.6 | convolution fusion | flops 4594335744 | bytes 14221824 | tf_op jit(solution)/shard_map/qt,cst->qcs/dot_general | solution.py:72
  85.7 2.7 copy.34
  88.5 59.0 %all_to_all.15 = bf16[8,2,32,128,32]{3,4,2,1,0:T(8,128)(2,1)S(1)} all-to-all(bf16[8,2,32,128,32]{3,4,2,1,0:T(8,128)(2,1)S(1)} %copy.34), channel_id=1, replica_groups=mesh['pair'=32,'win'=8] {'win'}, dimensions={0} | all-to-all | bytes 8388608 | tf_op jit(solution)/shard_map/all_to_all | solution.py:78
  147.5 3.3 %copy.58 = bf16[8,2,32,128,32]{3,4,0,2,1:T(8,128)(2,1)} copy(bf16[8,2,32,128,32]{3,4,2,1,0:T(8,128)(2,1)S(1)} %all_to_all.15) | data formatting | bytes 8388608 | tf_op jit(solution)/shard_map/all_to_all | solution.py:78
  150.8 6.3 %copy.36 = bf16[2,32,128,256]{3,2,1,0:T(8,128)(2,1)} copy(bf16[2,32,128,256]{2,3,1,0:T(8,128)(2,1)} %bitcast.67) | data formatting | bytes 8388608 | tf_op jit(solution)/shard_map/reshape | solution.py:79
  157.1 2.9 collective-permute-start.2
  160.0 36.6 %collective-permute-start.1 = (bf16[2,32,128,256]{3,2,1,0:T(8,128)(2,1)}, bf16[2,32,128,256]{3,2,1,0:T(8,128)(2,1)S(1)}, u32[]{:S(2)}, u32[]{:S(2)}) collective-permute-start(bf16[2,32,128,256]{3,2,1,0:T(8,128)(2,1)} %copy.36), channel_id=1, source_target_pairs={{0,8},{8,16},{16,24},{24,32},{32,40},{40,48},{48,56},{56,64},{64,7... | collective-permute-start | bytes 12582920 | tf_op jit(solution)/shard_map/ppermute | solution.py:20
  196.6 2.9 fusion.36
  199.6 94.8 %collective-permute-done.2 = bf16[2,32,128,256]{3,2,1,0:T(8,128)(2,1)S(1)} collective-permute-done((bf16[2,32,128,256]{3,2,1,0:T(8,128)(2,1)}, bf16[2,32,128,256]{3,2,1,0:T(8,128)(2,1)S(1)}, u32[]{:S(2)}, u32[]{:S(2)}) %collective-permute-start.2) | collective-permute-done | bytes 4194336 | tf_op jit(solution)/shard_map/ppermute | solution.py:20
  294.3 0.7 fusion.23
  295.1 0.8 fusion.24
  295.8 0.8 subtract_bitcast_fusion
  296.6 0.8 add_bitcast_fusion
  299.4 0.8 subtract_bitcast_fusion.1
  301.5 2.4 pad_maximum_fusion
  (16 shorter events, 4.9 us)
Async XLA Ops:
  12.1 14.5 %copy-start = (f32[64]{0:T(128)S(1)}, f32[64]{0:T(128)}, u32[]{:S(2)}) copy-start(f32[64]{0:T(128)} %param.4) | copy-start | bytes 772
  12.8 64.5 %collective-permute-start = (bf16[128,64]{0,1:T(8,128)(2,1)S(1)}, bf16[128,64]{0,1:T(8,128)(2,1)S(1)}, u32[]{:S(2)}, u32[]{:S(2)}) collective-permute-start(bf16[128,64]{0,1:T(8,128)(2,1)S(1)} %slice_bitcast_fusion.20), channel_id=1, source_target_pairs={{0,1},{1,2},{2,3},{3,4},{4,5},{5,6},{6,7},{8,9},{9,10},{10,11},{11... | collective-permute-start | bytes 49160 | tf_op jit(solution)/shard_map/ppermute | solution.py:14
  66.3 10.2 %copy-start.1 = (s32[128]{0:T(128)S(1)}, s32[128]{0:T(128)}, u32[]{:S(2)}) copy-start(s32[128]{0:T(128)} %param.5) | copy-start | bytes 1540
  157.1 137.2 %collective-permute-start.2 = (bf16[2,32,128,256]{3,2,1,0:T(8,128)(2,1)}, bf16[2,32,128,256]{3,2,1,0:T(8,128)(2,1)S(1)}, u32[]{:S(2)}, u32[]{:S(2)}) collective-permute-start(bf16[2,32,128,256]{3,2,1,0:T(8,128)(2,1)} %copy.36), channel_id=1, source_target_pairs={{0,128},{8,136},{16,144},{24,152},{32,160},{40,168},{48,176},{56,1... | collective-permute-start | bytes 12582920 | tf_op jit(solution)/shard_map/ppermute | solution.py:20
  160.0 137.9 %collective-permute-start.1 = (bf16[2,32,128,256]{3,2,1,0:T(8,128)(2,1)}, bf16[2,32,128,256]{3,2,1,0:T(8,128)(2,1)S(1)}, u32[]{:S(2)}, u32[]{:S(2)}) collective-permute-start(bf16[2,32,128,256]{3,2,1,0:T(8,128)(2,1)} %copy.36), channel_id=1, source_target_pairs={{0,8},{8,16},{16,24},{24,32},{32,40},{40,48},{48,56},{56,64},{64,7... | collective-permute-start | bytes 12582920 | tf_op jit(solution)/shard_map/ppermute | solution.py:20
where the time goes:
time: 306 us; the launch traced here: 304 us
  waiting for transfers between devices  94.8 us (31%)
  local copies, waits for them, and re-layouts  69.7 us (23%)
  blocking collectives  59 us (19%)
  starting transfers between devices  49.1 us (16%)
  matrix products  23.5 us (8%)
  other arithmetic  7.57 us (2%)
    ppermute x2, waiting for transfers between devices, shifted(): return lax.ppermute(value, axis, pairs)  94.8 us
    all_to_all x1, blocking collectives, per_device(): lax.all_to_all(spectra, 'win', split_axis=0, concat_axis=4, tiled=True)  59 us
    ppermute x2, starting transfers between devices, shifted(): return lax.ppermute(value, axis, pairs)  39.5 us
    another operation x2, local copies, waits for them, and re-layouts, filtered_basis(): tiled = jnp.tile(pattern, length)[:length * (period - 1)]  15.9 us
    reshape x1, local copies, waits for them, and re-layouts, filtered_basis(): filt = tiled.reshape(length, period - 1)[:, :samples]  15.5 us
    unnamed x5, local copies, waits for them, and re-layouts  12.1 us
    ppermute x1, starting transfers between devices, passed_along(): return lax.ppermute(block, axis, route)  9.63 us
    dot_general x1, matrix products, filtered_basis(): jnp.dot(filt, plain, preferred_element_type=jnp.float32, precision=lax.Pr...  9.12 us
  transfers between devices with their start and end apart: 3, of which 1 were waited for; matrix products, arithmetic and copies ran while one was open for 20% of the time, Pallas kernels for 0%

commit v1 on v0

v1 whole, which is shorter than its diff:
```python
import math

import jax
import jax.numpy as jnp
import numpy as np
from jax import lax
from jax.experimental import pallas as pl
from jax.experimental.pallas import tpu as pltpu
from jax.sharding import PartitionSpec as P

BINS = 256
SHARE = 32
CH = 128
SUBS = 32
SAMPLES = 1024
TAPS = 64
CHUNKS = 4
PER = SHARE // CHUNKS
MESH = pl.DeviceIdType.MESH
F32 = jnp.float32
BF16 = jnp.bfloat16
NT = (((1,), (1,)), ((), ()))
TN = (((0,), (0,)), ((), ()))


def tables():
    k = np.arange(BINS)[:, None]
    n = np.arange(SAMPLES)[None, :]
    phase = ((k * n) % SAMPLES) * (2.0 * math.pi / SAMPLES)
    return np.cos(phase).astype(np.float32), np.sin(phase).astype(np.float32)


def gather_matrix():
    m = np.zeros((256, 256), np.float32)
    for s in range(16):
        for ch in range(16):
            m[s * 16 + ch, ch * 16 + s] = 1.0
    return m


PIECES = ["own", 0, 1, 2, 3]


def part(ref, piece):
    if piece == "own":
        return ref.at[:, pl.ds(0, SUBS), :]
    return ref.at[pl.ds(PER * piece, PER), pl.ds(SUBS, 3 * SUBS), :]


def peers(ref, piece):
    return ref.at[pl.ds(PER * piece, PER)]


def sem_table():
    names = ["tail"]
    names += [("x", half, r, j) for half in (0, 1) for j in range(CHUNKS) for r in (1, 2, 3)]
    for kind in ("swap", "relay", "pass", "near", "far", "ynear", "yfar"):
        names += [(kind, piece) for piece in PIECES]
    return {name: i for i, name in enumerate(names)}


SEMS = sem_table()


def kernel(
    traces, taps, alive, cos_hbm, sin_hbm, perm, out,
    tv, ts, cosv, sinv, basis, acc, sp, own, pb0, pb1, swp, rly, rlp, outv,
    load_sem, out_sem, send_sem, recv_sem,
):
    pair, win = lax.axis_index("pair"), lax.axis_index("win")
    c, zl, y = lax.rem(pair, 2), lax.rem(pair // 2, 4), pair // 8
    x, hz = win // 2, lax.rem(win, 2)
    z = hz * 4 + zl

    def dev(dx, dy, dz, core):
        xx, yy, zz = lax.rem(x + dx + 4, 4), lax.rem(y + dy + 4, 4), lax.rem(z + dz + 8, 8)
        return {"pair": (yy * 4 + lax.rem(zz, 4)) * 2 + core, "win": xx * 2 + zz // 4}

    last = jnp.where(zl == 3, 1, 0)
    first = jnp.where(zl == 0, 1, 0)
    next_win = {"pair": pair, "win": lax.rem(win + 1, 8)}
    prev_win = {"pair": pair, "win": lax.rem(win + 7, 8)}
    swap_to = dev(0, last, -3 + 4 * last, 0)
    near_to = dev(0, last, 1 - 4 * last, 0)
    swap_from = dev(0, -first, 3 - 4 * first, 1)
    near_from = dev(0, -first, -1 + 4 * first, 1)

    barrier = pltpu.get_barrier_semaphore()
    same = [dev(r, 0, 0, c) for r in (1, 2, 3)] + [next_win, prev_win]
    same += [dev(0, 0, 2, c), dev(0, 0, -2, c), dev(0, 2, 0, c), dev(0, 0, 0, 1 - c)]
    for target in same:
        pl.semaphore_signal(barrier, inc=1, device_id=target, device_id_type=MESH)

    @pl.when(c == 0)
    def _():
        for target in (swap_from, near_from):
            pl.semaphore_signal(barrier, inc=1, device_id=target, device_id_type=MESH)

    @pl.when(c == 1)
    def _():
        for target in (swap_to, near_to):
            pl.semaphore_signal(barrier, inc=1, device_id=target, device_id_type=MESH)

    copies = [
        pltpu.make_async_copy(cos_hbm, cosv, load_sem.at[8]),
        pltpu.make_async_copy(sin_hbm, sinv, load_sem.at[9]),
    ]
    for copy in copies:
        copy.start()

    def load(g):
        rows = pl.ds(pl.multiple_of(g * 16, 16), 16)
        return pltpu.make_async_copy(traces.at[rows], tv.at[rows], load_sem.at[g])

    for g in range(8):
        load(g).start()
    for copy in copies:
        copy.wait()

    scale = 1.0 / math.sqrt(SAMPLES)
    tap_row = taps[0:1, :]
    lanes = lax.broadcasted_iota(jnp.int32, (128, 128), 1)
    rows = lax.broadcasted_iota(jnp.int32, (128, 128), 0)
    turned = pltpu.roll(jnp.broadcast_to(tap_row, (128, 128)), 0, 1, stride=1, stride_axis=0)
    edge = jnp.where((rows >= TAPS) & (lanes < rows - TAPS), turned, 0.0)
    for half in (0, 1):
        h = hz if half else 1 - hz
        for r in range(4):
            k0 = pl.multiple_of(SHARE * (2 * lax.rem(x + r, 4) + h), SHARE)
            head_cos = cosv[pl.ds(k0, SHARE), 0:128]
            head_sin = sinv[pl.ds(k0, SHARE), 0:128]
            hr = jnp.sum(head_cos * tap_row, axis=1, keepdims=True) * scale
            hi = -jnp.sum(head_sin * tap_row, axis=1, keepdims=True) * scale
            left_re = lax.dot_general(
                head_cos * scale, edge, NT, precision=lax.Precision.HIGHEST, preferred_element_type=F32
            )
            left_im = lax.dot_general(
                head_sin * -scale, edge, NT, precision=lax.Precision.HIGHEST, preferred_element_type=F32
            )
            for t in range(8):
                cs = cosv[pl.ds(k0, SHARE), 128 * t : 128 * t + 128]
                sn = sinv[pl.ds(k0, SHARE), 128 * t : 128 * t + 128]
                re = cs * hr + sn * hi
                im = cs * hi - sn * hr
                if t == 7:
                    re = re - left_re
                    im = im - left_im
                basis[half, 64 * r : 64 * r + 32, 128 * t : 128 * t + 128] = re.astype(BF16)
                basis[half, 64 * r + 32 : 64 * r + 64, 128 * t : 128 * t + 128] = im.astype(BF16)
            basis[half, 64 * r : 64 * r + 32, 1024:1152] = left_re.astype(BF16)
            basis[half, 64 * r + 32 : 64 * r + 64, 1024:1152] = left_im.astype(BF16)

    def regroup(g, carry):
        load(g).wait()
        chans = pl.ds(pl.multiple_of(g * 16, 16), 16)
        for sh in (0, 1):
            for t in range(4):
                cols = slice(256 * t, 256 * t + 256)
                block = tv[chans, 16 * sh : 16 * sh + 16, cols].reshape(256, 256)
                moved = jnp.dot(perm[...], block, preferred_element_type=F32).astype(BF16)
                ts[pl.ds(1 + 16 * sh, 16), chans, cols] = moved.reshape(16, 16, 256)
        return carry

    lax.fori_loop(0, 8, regroup, 0)

    pl.semaphore_wait(barrier, 11)

    def remote(name, src, dst, target, sent=None):
        return pltpu.make_async_remote_copy(
            src_ref=src, dst_ref=dst, send_sem=send_sem.at[SEMS[sent or name]], recv_sem=recv_sem.at[SEMS[name]],
            device_id=target, device_id_type=MESH,
        )

    tail = remote("tail", ts.at[SUBS, :, pl.ds(896, 128)], ts.at[0, :, pl.ds(896, 128)], next_win)
    tail.start()

    alive_row = jnp.concatenate([alive[0:1, :], alive[0:1, :]], axis=1)

    def transform(half, p):
        s0 = p * 2
        main = ts[pl.ds(s0 + 1, 2)].reshape(256, SAMPLES)
        prior = ts[pl.ds(s0, 2), :, 896:1024].reshape(256, 128)
        total = lax.dot_general(basis[half, :, 0:1024], main, NT, preferred_element_type=F32)
        total += lax.dot_general(basis[half, :, 1024:1152], prior, NT, preferred_element_type=F32)
        total = total * alive_row
        acc[pl.ds(s0, 256, stride=SUBS), :] = total[:, 0:128]
        acc[pl.ds(s0 + 1, 256, stride=SUBS), :] = total[:, 128:256]

    def pack(half, r):
        def one(i, carry):
            re = acc[pl.ds(pl.multiple_of((r * 64 + i) * SUBS, SUBS), SUBS), :].astype(BF16)
            im = acc[pl.ds(pl.multiple_of((r * 64 + 32 + i) * SUBS, SUBS), SUBS), :].astype(BF16)
            if half == 1 and r == 0:
                own[0, i, 0:SUBS, 0:128] = re
                own[0, i, 0:SUBS, 128:256] = im
            else:
                sp[half, r, i, :, 0:128] = re
                sp[half, r, i, :, 128:256] = im
            return carry

        lax.fori_loop(0, SHARE, one, 0, unroll=4)

    def transform_rest(half):
        def step(p, carry):
            transform(half, p)
            return carry

        lax.fori_loop(1, 16, step, 0)

    def x_copy(half, r, j):
        src = sp.at[half, r, pl.ds(PER * j, PER)]
        rows = pl.ds((3 - r) * SUBS, SUBS)
        if half == 0:
            dst = swp.at[pl.ds(PER * j, PER), rows, :]
        else:
            dst = own.at[0, pl.ds(PER * j, PER), pl.ds((4 - r) * SUBS, SUBS), :]
        return remote(("x", half, r, j), src, dst, dev(r, 0, 0, c))

    def swap_src(piece):
        return sp.at[0, 0] if piece == "own" else peers(swp, piece)

    def relay_buf(piece):
        return rly if piece == "own" else peers(rlp, piece)

    def turn(piece):
        return -2 if piece == 3 else 2

    def swap_even(piece):
        return remote(("relay", piece), swap_src(piece), relay_buf(piece), dev(0, 0, turn(piece), 0))

    def swap_even_on(piece):
        return remote(("swap", piece), relay_buf(piece), part(own.at[1], piece), dev(0, 0, turn(piece), 0))

    def swap_odd(piece):
        return remote(("far", piece), swap_src(piece), part(pb0.at[1], piece), swap_to)

    def swap_odd_on(piece):
        src, dst = part(pb0.at[1], piece), part(own.at[1], piece)
        return remote(("swap", piece), src, dst, dev(0, 0, -1, 1), ("pass", piece))

    def swap_odd_last(piece):
        return remote(("swap", piece), swap_src(piece), part(own.at[1], piece), dev(0, 0, 4, 1))

    def near_odd(piece):
        return remote(("near", piece), part(own.at[0], piece), part(pb0.at[0], piece), near_to)

    def near_even(piece):
        return remote(("near", piece), part(own.at[0], piece), part(pb0.at[0], piece), dev(0, 0, 0, 1))

    def far_even(piece):
        return remote(("far", piece), part(own.at[1], piece), part(pb0.at[1], piece), dev(0, 0, 0, 1))

    def y_copy(slot, piece):
        name = ("ynear" if slot == 0 else "yfar", piece)
        return remote(name, part(own.at[slot], piece), part(pb1.at[slot], piece), dev(0, 2, 0, c))

    even, odd = c == 0, c == 1

    def send_swap(piece):
        @pl.when(even)
        def _():
            swap_even(piece).start()

        @pl.when(odd)
        def _():
            swap_odd(piece).start()

            @pl.when(zl == 3)
            def _():
                swap_odd_last(piece).start()

    def send_near(piece):
        y_copy(0, piece).start()

        @pl.when(even)
        def _():
            near_even(piece).start()

    def send_near_odd(piece):
        @pl.when(odd)
        def _():
            near_odd(piece).start()

    def pass_on(piece):
        @pl.when(even)
        def _():
            swap_even(piece).wait_recv()
            swap_even_on(piece).start()
            swap_odd(piece).wait_recv()

            @pl.when(zl != 0)
            def _():
                swap_odd_on(piece).start()

    def send_far(piece):
        swap_even_on(piece).wait_recv()
        y_copy(1, piece).start()

        @pl.when(even)
        def _():
            far_even(piece).start()

    def x_done(half, j):
        for r in (1, 2, 3):
            x_copy(half, r, j).wait_recv()

    transform_rest(0)
    tail.wait_recv()

    @pl.when(win == 0)
    def _():
        ts[0, :, 896:1024] = jnp.zeros((CH, 128), BF16)

    transform(0, 0)
    pack(0, 0)
    send_swap("own")
    for r in (1, 2, 3):
        pack(0, r)
    for j in (0, 1):
        for r in (1, 2, 3):
            x_copy(0, r, j).start()
    transform_rest(1)
    transform(1, 0)
    pack(1, 0)
    send_near("own")
    for r in (1, 2, 3):
        pack(1, r)
    for half, j in ((1, 0), (0, 2), (1, 1), (0, 3), (1, 2), (1, 3)):
        for r in (1, 2, 3):
            x_copy(half, r, j).start()

    def stage_x(j):
        x_done(0, j)
        send_swap(j)
        x_done(1, j)
        send_near(j)

    norm = 1.0 / math.sqrt(SUBS * 8)

    def out_copy(j):
        bins = pl.ds(PER * j, PER)
        return pltpu.make_async_copy(outv.at[:, :, bins], out.at[:, :, bins], out_sem.at[j])

    def cross(j):
        for piece in ([j] if j else ["own", j]):
            y_copy(0, piece).wait_recv()
            y_copy(1, piece).wait_recv()
            near_even(piece).wait_recv()

            @pl.when(odd)
            def _():
                far_even(piece).wait_recv()

        def one(i, carry):
            f = PER * j + i
            mine = jnp.concatenate([own[0, f], own[1, f]], axis=0)
            for rnd, ref in ((0, pb0), (1, pb1)):
                other = jnp.concatenate([ref[0, f], ref[1, f]], axis=0)
                g = lax.dot_general(mine, other, TN, preferred_element_type=F32)
                re = (g[0:128, 0:128] + g[128:256, 128:256]) * norm
                im = (g[128:256, 0:128] - g[0:128, 128:256]) * norm
                outv[0, rnd, f] = re.astype(BF16)
                outv[1, rnd, f] = im.astype(BF16)
            return carry

        lax.fori_loop(0, PER, one, 0)
        out_copy(j).start()

    stage_x(0)
    stage_x(1)
    pass_on("own")
    stage_x(2)
    pass_on(0)
    send_far("own")
    stage_x(3)
    pass_on(1)
    send_far(0)
    send_near_odd("own")
    send_near_odd(0)
    pass_on(2)
    send_far(1)
    send_near_odd(1)
    cross(0)
    pass_on(3)
    send_far(2)
    send_near_odd(2)
    cross(1)
    send_far(3)
    send_near_odd(3)
    cross(2)
    cross(3)

    tail.wait_send()
    for half in (0, 1):
        for j in range(CHUNKS):
            for r in (1, 2, 3):
                x_copy(half, r, j).wait_send()
    for piece in PIECES:
        y_copy(0, piece).wait_send()
        y_copy(1, piece).wait_send()

        @pl.when(even)
        def _():
            swap_even(piece).wait_send()
            swap_even_on(piece).wait_send()
            near_even(piece).wait_send()
            far_even(piece).wait_send()

            @pl.when(zl != 0)
            def _():
                swap_odd_on(piece).wait_send()

        @pl.when(odd)
        def _():
            swap_odd(piece).wait_send()
            near_odd(piece).wait_send()

            @pl.when(zl == 3)
            def _():
                swap_odd_last(piece).wait_send()
    for j in range(CHUNKS):
        out_copy(j).wait()


def per_device(traces, taps, alive):
    cos, sin = tables()
    tap_row = jnp.pad(taps.astype(F32)[None, :], ((0, 0), (0, 128 - TAPS)))
    alive_row = alive.astype(F32)[None, :]
    n = len(SEMS)
    vmem = pl.BlockSpec(memory_space=pltpu.VMEM)
    hbm = pl.BlockSpec(memory_space=pl.ANY)
    half = (SHARE, 4 * SUBS, 256)
    return pl.pallas_call(
        kernel,
        out_shape=jax.ShapeDtypeStruct((2, 2, SHARE, CH, CH), BF16),
        in_specs=[hbm, vmem, vmem, hbm, hbm, vmem],
        out_specs=hbm,
        scratch_shapes=[
            pltpu.VMEM((CH, SUBS, SAMPLES), BF16),
            pltpu.VMEM((SUBS + 1, CH, SAMPLES), BF16),
            pltpu.VMEM((BINS, SAMPLES), F32),
            pltpu.VMEM((BINS, SAMPLES), F32),
            pltpu.VMEM((2, 256, SAMPLES + 128), BF16),
            pltpu.VMEM((256 * SUBS, 128), F32),
            pltpu.VMEM((2, 4, SHARE, SUBS, 256), BF16),
            pltpu.VMEM((2,) + half, BF16),
            pltpu.VMEM((2,) + half, BF16),
            pltpu.VMEM((2,) + half, BF16),
            pltpu.VMEM((SHARE, 3 * SUBS, 256), BF16),
            pltpu.VMEM((SHARE, SUBS, 256), BF16),
            pltpu.VMEM((SHARE, 3 * SUBS, 256), BF16),
            pltpu.VMEM((2, 2, SHARE, CH, CH), BF16),
            pltpu.SemaphoreType.DMA((10,)),
            pltpu.SemaphoreType.DMA((CHUNKS,)),
            pltpu.SemaphoreType.DMA((n,)),
            pltpu.SemaphoreType.DMA((n,)),
        ],
        compiler_params=pltpu.CompilerParams(
            collective_id=0, has_side_effects=True, vmem_limit_bytes=60 * 2**20
        ),
        cost_estimate=pl.CostEstimate(flops=7 * 10**9, bytes_accessed=16 * 2**20, transcendentals=0),
    )(traces, tap_row, alive_row, jnp.asarray(cos), jnp.asarray(sin), jnp.asarray(gather_matrix(), BF16))


def solution(mesh):
    return jax.shard_map(
        per_device,
        mesh=mesh,
        in_specs=(P("pair", "win", None), P(), P("pair")),
        out_specs=P(None, None, "win", "pair", None),
        check_vma=False,
    )
```

time: 306 us -> 184 us (0.60)
  Pallas kernels: 0 us -> 176 us
  waiting for transfers between devices: 94.8 us -> 0 us
  local copies, waits for them, and re-layouts: 69.7 us -> 5.96 us
  blocking collectives: 59 us -> 0 us
  starting transfers between devices: 49.1 us -> 0 us
  matrix products: 23.5 us -> 0 us
  other arithmetic: 7.57 us -> 1.17 us
    pallas_call x0 -> x1, Pallas kernels: none -> 176 us  [per_device(): pl.pallas_call(kernel, out_shape=jax.ShapeDtypeStruct((2, 2, SHARE, CH, C...]
    ppermute x3 -> x0, waiting for transfers between devices: 94.8 us -> none  [the longest x2 94.8 us: shifted(): return lax.ppermute(value, axis, pairs)]
    all_to_all x1 -> x0, blocking collectives: 59 us -> none  [per_device(): lax.all_to_all(spectra, 'win', split_axis=0, concat_axis=4, tiled=True)]
    ppermute x3 -> x0, starting transfers between devices: 49.1 us -> none  [the longest x2 39.5 us: shifted(): return lax.ppermute(value, axis, pairs)]
    reshape x3 -> x0, local copies, waits for them, and re-layouts: 24.5 us -> none  [the longest x1 15.5 us: filtered_basis(): filt = tiled.reshape(length, period - 1)[:, :samples]]
    dot_general x10 -> x0, matrix products: 23.5 us -> none  [the longest x1 9.12 us: filtered_basis(): jnp.dot(filt, plain, preferred_element_type=jnp.float32, precision=lax.Pr...]
    another operation x2 -> x0, local copies, waits for them, and re-layouts: 15.9 us -> none  [filtered_basis(): tiled = jnp.tile(pattern, length)[:length * (period - 1)]]
    slice x3 -> x0, local copies, waits for them, and re-layouts: 12.3 us -> none  [the longest x1 8.26 us: filtered_basis(): tiled = jnp.tile(pattern, length)[:length * (period - 1)]]
  transfers between devices with their start and end apart: 3 -> 0, of which waited for: 1 -> 0; matrix products, arithmetic and copies ran while one was open for 20% -> 0% of each run, Pallas kernels for 0% -> 0%
where the time goes in v1:
time: 184 us; the launch traced here: 183 us
  Pallas kernels  176 us (96%)
  local copies, waits for them, and re-layouts  5.96 us (3%)
    pallas_call x1, Pallas kernels, per_device(): pl.pallas_call(kernel, out_shape=jax.ShapeDtypeStruct((2, 2, SHARE, CH, C...  176 us
    unnamed x1, local copies, waits for them, and re-layouts  4.79 us

profile of v1, /device:TPU:1, one launch (start us, length us, event | category | flops | bytes accessed | tf_op | source)
XLA Modules:
  0.0 183.4 jit_solution(3436944925716822371)
XLA Ops:
  0.0 1.2 pad.4.taps
  1.2 1.2 convert_bitcast_fusion.alive
  2.3 176.3 %shard_map.64 = bf16[2,2,32,128,128]{4,3,2,1,0:T(8,128)(2,1)} custom-call(bf16[128,32,1024]{2,1,0:T(8,128)(2,1)} %traces.1, f32[1,128]{1,0:T(1,128)} %pad.4.taps, f32[1,128]{1,0:T(1,128)} %convert_bitcast_fusion.alive, f32[256,1024]{1,0:T(8,128)} %constant.9.clone.cos_hbm, f32[256,1024]{1,0:T(8,128)} %constant.10.clone.sin_hbm, ...), custom_call_target="tpu_custom_call" | custom-call | flops 7000000000 | bytes 16777216 | tf_op jit(solution)/shard_map/pallas_call | solution.py:433
  178.6 4.8 %copy.8 = bf16[2,2,32,128,128]{4,3,2,1,0:T(8,128)(2,1)} copy(bf16[2,2,32,128,128]{4,3,2,1,0:T(8,128)(2,1)} %shard_map.64) | data formatting | bytes 8388608

commit v2 on v1

--- a/solution.py
+++ b/solution.py
@@ -39,6 +39,7 @@
 
 
 PIECES = ["own", 0, 1, 2, 3]
+STEERED = 3
 
 
 def part(ref, piece):
@@ -54,7 +55,7 @@
 def sem_table():
     names = ["tail"]
     names += [("x", half, r, j) for half in (0, 1) for j in range(CHUNKS) for r in (1, 2, 3)]
-    for kind in ("swap", "relay", "pass", "near", "far", "ynear", "yfar"):
+    for kind in ("swap", "relay", "pass", "near", "far", "ynear", "yfar", "yrelay", "last"):
         names += [(kind, piece) for piece in PIECES]
     return {name: i for i, name in enumerate(names)}
 
@@ -64,7 +65,7 @@
 
 def kernel(
     traces, taps, alive, cos_hbm, sin_hbm, perm, out,
-    tv, ts, cosv, sinv, basis, acc, sp, own, pb0, pb1, swp, rly, rlp, outv,
+    tv, ts, cosv, sinv, basis, acc, sp, own, pb0, pb1, swp, rly, rlp, outv, yrest,
     load_sem, out_sem, send_sem, recv_sem,
 ):
     pair, win = lax.axis_index("pair"), lax.axis_index("win")
@@ -76,30 +77,17 @@
         xx, yy, zz = lax.rem(x + dx + 4, 4), lax.rem(y + dy + 4, 4), lax.rem(z + dz + 8, 8)
         return {"pair": (yy * 4 + lax.rem(zz, 4)) * 2 + core, "win": xx * 2 + zz // 4}
 
-    last = jnp.where(zl == 3, 1, 0)
-    first = jnp.where(zl == 0, 1, 0)
     next_win = {"pair": pair, "win": lax.rem(win + 1, 8)}
     prev_win = {"pair": pair, "win": lax.rem(win + 7, 8)}
-    swap_to = dev(0, last, -3 + 4 * last, 0)
-    near_to = dev(0, last, 1 - 4 * last, 0)
-    swap_from = dev(0, -first, 3 - 4 * first, 1)
-    near_from = dev(0, -first, -1 + 4 * first, 1)
-
     barrier = pltpu.get_barrier_semaphore()
+    side = 2 * c - 1
     same = [dev(r, 0, 0, c) for r in (1, 2, 3)] + [next_win, prev_win]
-    same += [dev(0, 0, 2, c), dev(0, 0, -2, c), dev(0, 2, 0, c), dev(0, 0, 0, 1 - c)]
+    same += [dev(0, 2, 0, c), dev(0, 0, 0, 1 - c)]
+    same += [dev(0, 1, 0, c), dev(0, -1, 0, c)]
+    same += [dev(0, 0, -3 * side, 1 - c), dev(0, 0, side, 1 - c)]
+    same += [dev(0, side, side, 1 - c), dev(0, side, 0, 1 - c), dev(0, 0, 3, c), dev(0, 0, -3, c)]
     for target in same:
         pl.semaphore_signal(barrier, inc=1, device_id=target, device_id_type=MESH)
-
-    @pl.when(c == 0)
-    def _():
-        for target in (swap_from, near_from):
-            pl.semaphore_signal(barrier, inc=1, device_id=target, device_id_type=MESH)
-
-    @pl.when(c == 1)
-    def _():
-        for target in (swap_to, near_to):
-            pl.semaphore_signal(barrier, inc=1, device_id=target, device_id_type=MESH)
 
     copies = [
         pltpu.make_async_copy(cos_hbm, cosv, load_sem.at[8]),
@@ -118,7 +106,7 @@
         copy.wait()
 
     scale = 1.0 / math.sqrt(SAMPLES)
-    tap_row = taps[0:1, :]
+    tap_row = jnp.concatenate([taps[0:1, :], jnp.zeros((1, 128 - TAPS), F32)], axis=1)
     lanes = lax.broadcasted_iota(jnp.int32, (128, 128), 1)
     rows = lax.broadcasted_iota(jnp.int32, (128, 128), 0)
     turned = pltpu.roll(jnp.broadcast_to(tap_row, (128, 128)), 0, 1, stride=1, stride_axis=0)
@@ -163,7 +151,7 @@
 
     lax.fori_loop(0, 8, regroup, 0)
 
-    pl.semaphore_wait(barrier, 11)
+    pl.semaphore_wait(barrier, 15)
 
     def remote(name, src, dst, target, sent=None):
         return pltpu.make_async_remote_copy(
@@ -174,7 +162,8 @@
     tail = remote("tail", ts.at[SUBS, :, pl.ds(896, 128)], ts.at[0, :, pl.ds(896, 128)], next_win)
     tail.start()
 
-    alive_row = jnp.concatenate([alive[0:1, :], alive[0:1, :]], axis=1)
+    alive_row = alive[0:1, :].astype(F32)
+    alive_row = jnp.concatenate([alive_row, alive_row], axis=1)
 
     def transform(half, p):
         s0 = p * 2
@@ -222,27 +211,40 @@
     def relay_buf(piece):
         return rly if piece == "own" else peers(rlp, piece)
 
-    def turn(piece):
-        return -2 if piece == 3 else 2
-
     def swap_even(piece):
-        return remote(("relay", piece), swap_src(piece), relay_buf(piece), dev(0, 0, turn(piece), 0))
+        return remote(("relay", piece), swap_src(piece), relay_buf(piece), dev(0, 0, 3, 1))
 
     def swap_even_on(piece):
-        return remote(("swap", piece), relay_buf(piece), part(own.at[1], piece), dev(0, 0, turn(piece), 0))
+        return remote(("swap", piece), relay_buf(piece), part(own.at[1], piece), dev(0, 0, 1, 0), ("relay", piece))
 
     def swap_odd(piece):
-        return remote(("far", piece), swap_src(piece), part(pb0.at[1], piece), swap_to)
+        return remote(("far", piece), swap_src(piece), part(pb0.at[1], piece), dev(0, 0, -3, 0))
 
     def swap_odd_on(piece):
         src, dst = part(pb0.at[1], piece), part(own.at[1], piece)
         return remote(("swap", piece), src, dst, dev(0, 0, -1, 1), ("pass", piece))
 
-    def swap_odd_last(piece):
-        return remote(("swap", piece), swap_src(piece), part(own.at[1], piece), dev(0, 0, 4, 1))
+    def swap_last(piece):
+        return remote(("relay", piece), swap_src(piece), relay_buf(piece), dev(0, 0, -3, 0), ("far", piece))
+
+    def swap_last_on(piece):
+        src, dst = relay_buf(piece), part(own.at[1], piece)
+        return remote(("swap", piece), src, dst, dev(0, 0, -1, 1), ("pass", piece))
+
+    def far_last(piece):
+        src, dst = swap_src(piece), part(pb0.at[1], piece)
+        return remote(("far", piece), src, dst, dev(0, 1, 1, 0), ("swap", piece))
 
     def near_odd(piece):
-        return remote(("near", piece), part(own.at[0], piece), part(pb0.at[0], piece), near_to)
+        return remote(("near", piece), part(own.at[0], piece), part(pb0.at[0], piece), dev(0, 0, 1, 0))
+
+    def near_last(piece):
+        src = part(own.at[0], piece)
+        return remote(("relay", piece), src, relay_buf(piece), dev(0, 1, 0, 0), ("near", piece))
+
+    def near_last_on(piece):
+        src, dst = relay_buf(piece), part(pb0.at[0], piece)
+        return remote(("near", piece), src, dst, dev(0, 0, -3, 0), ("last", piece))
 
     def near_even(piece):
         return remote(("near", piece), part(own.at[0], piece), part(pb0.at[0], piece), dev(0, 0, 0, 1))
@@ -254,6 +256,16 @@
         name = ("ynear" if slot == 0 else "yfar", piece)
         return remote(name, part(own.at[slot], piece), part(pb1.at[slot], piece), dev(0, 2, 0, c))
 
+    def y_first(piece):
+        return remote(("yrelay", piece), part(own.at[1], piece), yrest, dev(0, -1, 0, c))
+
+    def y_second(piece):
+        return remote(("yfar", piece), yrest, part(pb1.at[1], piece), dev(0, -1, 0, c))
+
+    def y_pass(piece):
+        y_first(piece).wait_recv()
+        y_second(piece).start()
+
     even, odd = c == 0, c == 1
 
     def send_swap(piece):
@@ -261,13 +273,13 @@
         def _():
             swap_even(piece).start()
 
-        @pl.when(odd)
+        @pl.when(odd & (zl != 3))
         def _():
             swap_odd(piece).start()
 
-            @pl.when(zl == 3)
-            def _():
-                swap_odd_last(piece).start()
+        @pl.when(odd & (zl == 3))
+        def _():
+            swap_last(piece).start()
 
     def send_near(piece):
         y_copy(0, piece).start()
@@ -276,25 +288,48 @@
         def _():
             near_even(piece).start()
 
+        @pl.when(odd & (zl == 3))
+        def _():
+            near_last(piece).start()
+
     def send_near_odd(piece):
+        @pl.when(odd & (zl != 3))
+        def _():
+            near_odd(piece).start()
+
+        @pl.when(odd & (zl == 3))
+        def _():
+            far_last(piece).start()
+
+        @pl.when(even & (zl == 3))
+        def _():
+            near_last(piece).wait_recv()
+            near_last_on(piece).start()
+
+    def pass_even(piece):
         @pl.when(odd)
-        def _():
-            near_odd(piece).start()
-
-    def pass_on(piece):
-        @pl.when(even)
         def _():
             swap_even(piece).wait_recv()
             swap_even_on(piece).start()
+
+    def pass_odd(piece):
+        @pl.when(even & (zl != 0))
+        def _():
             swap_odd(piece).wait_recv()
-
-            @pl.when(zl != 0)
-            def _():
-                swap_odd_on(piece).start()
+            swap_odd_on(piece).start()
+
+        @pl.when(even & (zl == 0))
+        def _():
+            swap_last(piece).wait_recv()
+            swap_last_on(piece).start()
+
+    def pass_on(piece):
+        pass_even(piece)
+        pass_odd(piece)
 
     def send_far(piece):
         swap_even_on(piece).wait_recv()
-        y_copy(1, piece).start()
+        (y_first(piece) if piece == STEERED else y_copy(1, piece)).start()
 
         @pl.when(even)
         def _():
@@ -329,9 +364,11 @@
         for r in (1, 2, 3):
             x_copy(half, r, j).start()
 
-    def stage_x(j):
+    def ax(j):
         x_done(0, j)
         send_swap(j)
+
+    def bx(j):
         x_done(1, j)
         send_near(j)
 
@@ -347,7 +384,7 @@
             y_copy(1, piece).wait_recv()
             near_even(piece).wait_recv()
 
-            @pl.when(odd)
+            @pl.when(odd | (zl == 0))
             def _():
                 far_even(piece).wait_recv()
 
@@ -366,27 +403,32 @@
         lax.fori_loop(0, PER, one, 0)
         out_copy(j).start()
 
-    stage_x(0)
-    stage_x(1)
-    pass_on("own")
-    stage_x(2)
+    ax(0)
+    ax(1)
+    pass_on('own')
+    bx(0)
+    ax(2)
+    bx(1)
     pass_on(0)
-    send_far("own")
-    stage_x(3)
+    ax(3)
+    bx(2)
+    bx(3)
     pass_on(1)
+    send_far('own')
+    pass_on(2)
     send_far(0)
-    send_near_odd("own")
+    pass_on(3)
+    send_near_odd('own')
     send_near_odd(0)
-    pass_on(2)
+    send_near_odd(1)
+    send_near_odd(2)
+    send_near_odd(3)
     send_far(1)
-    send_near_odd(1)
+    send_far(2)
     cross(0)
-    pass_on(3)
-    send_far(2)
-    send_near_odd(2)
+    send_far(3)
     cross(1)
-    send_far(3)
-    send_near_odd(3)
+    y_pass(3)
     cross(2)
     cross(3)
 
@@ -398,34 +440,36 @@
     for piece in PIECES:
         y_copy(0, piece).wait_send()
         y_copy(1, piece).wait_send()
+        if piece == STEERED:
+            y_first(piece).wait_send()
 
         @pl.when(even)
         def _():
             swap_even(piece).wait_send()
-            swap_even_on(piece).wait_send()
             near_even(piece).wait_send()
             far_even(piece).wait_send()
 
-            @pl.when(zl != 0)
+            swap_odd_on(piece).wait_send()
+
+            @pl.when(zl == 3)
             def _():
-                swap_odd_on(piece).wait_send()
+                near_last_on(piece).wait_send()
 
         @pl.when(odd)
         def _():
+            swap_even_on(piece).wait_send()
             swap_odd(piece).wait_send()
             near_odd(piece).wait_send()
 
             @pl.when(zl == 3)
             def _():
-                swap_odd_last(piece).wait_send()
+                far_last(piece).wait_send()
     for j in range(CHUNKS):
         out_copy(j).wait()
 
 
 def per_device(traces, taps, alive):
     cos, sin = tables()
-    tap_row = jnp.pad(taps.astype(F32)[None, :], ((0, 0), (0, 128 - TAPS)))
-    alive_row = alive.astype(F32)[None, :]
     n = len(SEMS)
     vmem = pl.BlockSpec(memory_space=pltpu.VMEM)
     hbm = pl.BlockSpec(memory_space=pl.ANY)
@@ -450,6 +494,7 @@
             pltpu.VMEM((SHARE, SUBS, 256), BF16),
             pltpu.VMEM((SHARE, 3 * SUBS, 256), BF16),
             pltpu.VMEM((2, 2, SHARE, CH, CH), BF16),
+            pltpu.VMEM((PER, 3 * SUBS, 256), BF16),
             pltpu.SemaphoreType.DMA((10,)),
             pltpu.SemaphoreType.DMA((CHUNKS,)),
             pltpu.SemaphoreType.DMA((n,)),
@@ -459,7 +504,7 @@
             collective_id=0, has_side_effects=True, vmem_limit_bytes=60 * 2**20
         ),
         cost_estimate=pl.CostEstimate(flops=7 * 10**9, bytes_accessed=16 * 2**20, transcendentals=0),
-    )(traces, tap_row, alive_row, jnp.asarray(cos), jnp.asarray(sin), jnp.asarray(gather_matrix(), BF16))
+    )(traces, taps[None, :], alive[None, :], jnp.asarray(cos), jnp.asarray(sin), jnp.asarray(gather_matrix(), BF16))
 
 
 def solution(mesh):

time: 184 us -> 161 us (0.88)
  Pallas kernels: 176 us -> 154 us
    pallas_call x1, Pallas kernels: 176 us -> 154 us  [per_device(): pl.pallas_call(kernel, out_shape=jax.ShapeDtypeStruct((2, 2, SHARE, CH, C...]
where the time goes in v2:
time: 161 us; the launch traced here: 159 us
  Pallas kernels  154 us (96%)
  local copies, waits for them, and re-layouts  4.79 us (3%)
    pallas_call x1, Pallas kernels, per_device(): pl.pallas_call(kernel, out_shape=jax.ShapeDtypeStruct((2, 2, SHARE, CH, C...  154 us
    unnamed x1, local copies, waits for them, and re-layouts  4.79 us

profile of v2, /device:TPU:1, one launch (start us, length us, event | category | flops | bytes accessed | tf_op | source)
XLA Modules:
  0.0 159.0 jit_solution(16675251236068719121)
XLA Ops:
  0.0 154.3 %shard_map.64 = bf16[2,2,32,128,128]{4,3,2,1,0:T(8,128)(2,1)} custom-call(bf16[128,32,1024]{2,1,0:T(8,128)(2,1)} %traces.1, f32[1,64]{1,0:T(1,128)} %bitcast.2, s32[1,128]{1,0:T(1,128)} %bitcast.3, f32[256,1024]{1,0:T(8,128)} %constant.6.clone.cos_hbm, f32[256,1024]{1,0:T(8,128)} %constant.7.clone.sin_hbm, bf16[256,256]{1,0:T(8,128)(2,1)} %constant.8.clone.perm), custom_call_target="tpu_custom_call" | custom-call | flops 7000000000 | bytes 16777216 | tf_op jit(solution)/shard_map/pallas_call | solution.py:477
  154.3 4.8 %copy.8 = bf16[2,2,32,128,128]{4,3,2,1,0:T(8,128)(2,1)} copy(bf16[2,2,32,128,128]{4,3,2,1,0:T(8,128)(2,1)} %shard_map.64) | data formatting | bytes 8388608

commit v3 on v2

--- a/solution.py
+++ b/solution.py
@@ -39,7 +39,7 @@
 
 
 PIECES = ["own", 0, 1, 2, 3]
-STEERED = 3
+STEERED = 2
 
 
 def part(ref, piece):
@@ -64,7 +64,7 @@
 
 
 def kernel(
-    traces, taps, alive, cos_hbm, sin_hbm, perm, out,
+    traces, taps, alive, cos_hbm, sin_hbm, perm, out_re, out_im,
     tv, ts, cosv, sinv, basis, acc, sp, own, pb0, pb1, swp, rly, rlp, outv, yrest,
     load_sem, out_sem, send_sem, recv_sem,
 ):
@@ -187,7 +187,7 @@
                 sp[half, r, i, :, 128:256] = im
             return carry
 
-        lax.fori_loop(0, SHARE, one, 0, unroll=4)
+        lax.fori_loop(0, SHARE, one, 0, unroll=16)
 
     def transform_rest(half):
         def step(p, carry):
@@ -297,10 +297,12 @@
         def _():
             near_odd(piece).start()
 
+    def send_far_last(piece):
         @pl.when(odd & (zl == 3))
         def _():
             far_last(piece).start()
 
+    def send_near_last(piece):
         @pl.when(even & (zl == 3))
         def _():
             near_last(piece).wait_recv()
@@ -376,7 +378,10 @@
 
     def out_copy(j):
         bins = pl.ds(PER * j, PER)
-        return pltpu.make_async_copy(outv.at[:, :, bins], out.at[:, :, bins], out_sem.at[j])
+        return [
+            pltpu.make_async_copy(outv.at[k, :, bins], ref.at[:, bins], out_sem.at[j, k])
+            for k, ref in ((0, out_re), (1, out_im))
+        ]
 
     def cross(j):
         for piece in ([j] if j else ["own", j]):
@@ -401,7 +406,8 @@
             return carry
 
         lax.fori_loop(0, PER, one, 0)
-        out_copy(j).start()
+        for copy in out_copy(j):
+            copy.start()
 
     ax(0)
     ax(1)
@@ -414,21 +420,31 @@
     bx(2)
     bx(3)
     pass_on(1)
+    send_near_last('own')
+    send_far_last('own')
     send_far('own')
     pass_on(2)
+    send_near_last(0)
+    send_far_last(0)
     send_far(0)
     pass_on(3)
+    send_near_last(1)
     send_near_odd('own')
     send_near_odd(0)
     send_near_odd(1)
     send_near_odd(2)
     send_near_odd(3)
+    send_far_last(1)
+    send_far_last(2)
+    send_far_last(3)
     send_far(1)
+    send_near_last(2)
     send_far(2)
+    send_near_last(3)
     cross(0)
     send_far(3)
     cross(1)
-    y_pass(3)
+    y_pass(2)
     cross(2)
     cross(3)
 
@@ -465,7 +481,8 @@
             def _():
                 far_last(piece).wait_send()
     for j in range(CHUNKS):
-        out_copy(j).wait()
+        for copy in out_copy(j):
+            copy.wait()
 
 
 def per_device(traces, taps, alive):
@@ -474,11 +491,12 @@
     vmem = pl.BlockSpec(memory_space=pltpu.VMEM)
     hbm = pl.BlockSpec(memory_space=pl.ANY)
     half = (SHARE, 4 * SUBS, 256)
-    return pl.pallas_call(
+    result = jax.ShapeDtypeStruct((2, SHARE, CH, CH), BF16)
+    parts = pl.pallas_call(
         kernel,
-        out_shape=jax.ShapeDtypeStruct((2, 2, SHARE, CH, CH), BF16),
+        out_shape=(result, result),
         in_specs=[hbm, vmem, vmem, hbm, hbm, vmem],
-        out_specs=hbm,
+        out_specs=(hbm, hbm),
         scratch_shapes=[
             pltpu.VMEM((CH, SUBS, SAMPLES), BF16),
             pltpu.VMEM((SUBS + 1, CH, SAMPLES), BF16),
@@ -496,7 +514,7 @@
             pltpu.VMEM((2, 2, SHARE, CH, CH), BF16),
             pltpu.VMEM((PER, 3 * SUBS, 256), BF16),
             pltpu.SemaphoreType.DMA((10,)),
-            pltpu.SemaphoreType.DMA((CHUNKS,)),
+            pltpu.SemaphoreType.DMA((CHUNKS, 2)),
             pltpu.SemaphoreType.DMA((n,)),
             pltpu.SemaphoreType.DMA((n,)),
         ],
@@ -505,6 +523,7 @@
         ),
         cost_estimate=pl.CostEstimate(flops=7 * 10**9, bytes_accessed=16 * 2**20, transcendentals=0),
     )(traces, taps[None, :], alive[None, :], jnp.asarray(cos), jnp.asarray(sin), jnp.asarray(gather_matrix(), BF16))
+    return jnp.stack(parts, axis=0)
 
 
 def solution(mesh):

time: 161 us -> 155 us (0.963)
  local copies, waits for them, and re-layouts: 4.79 us -> 0 us
  other arithmetic: 0 us -> 4.62 us
  Pallas kernels: 154 us -> 150 us
    unnamed x1 -> x0, local copies, waits for them, and re-layouts: 4.79 us -> none
    another operation x0 -> x1, other arithmetic: none -> 4.62 us  [per_device(): return jnp.stack(parts, axis=0)]
    pallas_call x1, Pallas kernels: 154 us -> 150 us  [per_device(): pl.pallas_call(kernel, out_shape=(result, result), in_specs=[hbm, vmem, v...]
where the time goes in v3:
time: 155 us; the launch traced here: 154 us
  Pallas kernels  150 us (97%)
  other arithmetic  4.62 us (3%)
    pallas_call x1, Pallas kernels, per_device(): pl.pallas_call(kernel, out_shape=(result, result), in_specs=[hbm, vmem, v...  150 us
    another operation x1, other arithmetic, per_device(): return jnp.stack(parts, axis=0)  4.62 us

profile of v3, /device:TPU:1, one launch (start us, length us, event | category | flops | bytes accessed | tf_op | source)
XLA Modules:
  0.0 154.4 jit_solution(8787045119570676971)
XLA Ops:
  0.0 149.8 %shard_map.64 = (bf16[2,32,128,128]{3,2,1,0:T(8,128)(2,1)}, bf16[2,32,128,128]{3,2,1,0:T(8,128)(2,1)}) custom-call(bf16[128,32,1024]{2,1,0:T(8,128)(2,1)} %traces.1, f32[1,64]{1,0:T(1,128)} %bitcast.6, s32[1,128]{1,0:T(1,128)} %bitcast.7, f32[256,1024]{1,0:T(8,128)} %constant.6.clone.cos_hbm, f32[256,1024]{1,0:T(8,128)} %constant.7.clone.sin_hbm, ...), custom_call_target="tpu_custom_call" | custom-call | flops 7000000000 | bytes 16777216 | tf_op jit(solution)/shard_map/pallas_call | solution.py:495
  149.8 4.6 %pad_maximum_fusion = bf16[2,2,32,128,128]{4,3,2,1,0:T(8,128)(2,1)} fusion(bf16[1,2,32,128,128]{4,3,2,1,0:T(8,128)(2,1)} %bitcast.5, bf16[1,2,32,128,128]{4,3,2,1,0:T(8,128)(2,1)} %bitcast.4), kind=kLoop, calls=%fused_computation | loop fusion | flops 2097152 | bytes 8388608 | tf_op jit(solution)/shard_map/stack | solution.py:526
